TPU v7x, 32 devices: a whole 2x2x4 slice. The times are simulated.
32 devices in a mesh: wide: 8 (over y, x, core), narrow: 4 (over z).
Axes of the slice: x: 2, y: 2, z: 4, core: 2. Of those that a mesh axis runs over, the one named last changes fastest.
Arguments:
- hidden: bfloat16 [2048, 2048], P(('wide', 'narrow')), may hold values from -6 to 6
- cotangent: bfloat16 [2048, 2048], P(('wide', 'narrow')), may hold values from -6 to 6
- routes: int32 [2048, 6], P(('wide', 'narrow')), may hold values from 0 to 15, all different within a row; in each aligned block of 64 rows (0 to 63, 64 to 127, ...) at most 48 rows name the same one
- gates: float32 [2048, 6], P(('wide', 'narrow')), may hold values from 0.05 to 1
- offsets: int32 [8], replicated, may hold values from 0 to 7, each once
- w_gate: bfloat16 [32, 2048, 704], P(('wide', 'narrow')), may hold values from -0.125 to 0.125
- w_up: bfloat16 [32, 2048, 704], P(('wide', 'narrow')), may hold values from -0.125 to 0.125
- w_down: bfloat16 [32, 704, 2048], P(('wide', 'narrow')), may hold values from -0.15625 to 0.15625
- w_out: bfloat16 [2048, 2048], P('narrow'), may hold values from -0.125 to 0.125
- latent: bfloat16 [2048, 512], P('wide'), may hold values from -6 to 6
- rope_key: bfloat16 [2048, 64], P('wide'), may hold values from -4 to 4
- q_nope: bfloat16 [2048, 2048], P('wide', 'narrow'), may hold values from -24 to 24
- q_pe: bfloat16 [2048, 1024], P('wide', 'narrow'), may hold values from -100 to 100
- w_uk: bfloat16 [2048, 512], P('narrow'), may hold values from -0.5 to 0.5
- w_uv: bfloat16 [2048, 512], P('narrow'), may hold values from -0.5 to 0.5
Outputs:
- resid_grad: bfloat16 [2048, 2048], P(('wide', 'narrow'))
- grad_q_nope: bfloat16 [2048, 2048], P('wide', 'narrow')
- grad_q_pe: bfloat16 [2048, 1024], P('wide', 'narrow')
- grad_latent: float32 [2048, 512], P(('wide', 'narrow'))
- grad_rope_key: float32 [2048, 64], P(('wide', 'narrow'))
Inputs may be any that keep to these rules, and one draw needn't show every extreme that they name: `routes`: each row names 6 different experts; in each aligned block of 64 rows no expert is named by more than 48 rows, and in some blocks one is named by exactly 48. A permutation of the sequence blocks: token i of block b stands at position offsets[b] * 256 + i.
All inputs are finite; a program needn't handle non-finite values.
Results may differ from a plain program's by a relative error of at most 0.028.
Values may be sent and summed in bfloat16 or wider, within the bound.
No kernel may reach another device: no remote copies, remote signals or barrier semaphores. Data moves between devices by JAX's collectives and lax.ppermute only.
A program may use at most 128 MiB of HBM per device.

v0:
```python
import math

import jax
import jax.numpy as jnp
from jax import lax
from jax.sharding import PartitionSpec as P

LATENT = 512
NOPE = 128
ROPE = 64
VDIM = 128


def swapped(value, axis, distance):
    mask = 2**distance
    pairs = [(source, source ^ mask) for source in range(lax.axis_size(axis))]
    return lax.ppermute(value, axis, pairs)


def slot_numbers(expert_ids, experts):
    onehot = (expert_ids[:, None] == jnp.arange(experts, dtype=jnp.int32)[None, :]).astype(
        jnp.int32
    )
    before = jnp.cumsum(onehot, axis=0) - onehot
    return jnp.sum(before * onehot, axis=1)


def on_device(
    hidden,
    cotangent,
    routes,
    gates,
    offsets,
    w_gate,
    w_up,
    w_down,
    w_out,
    latent,
    rope_key,
    q_nope,
    q_pe,
    w_uk,
    w_uv,
):
    tok_rows, model_width = hidden.shape
    top_count = routes.shape[1]
    devices = lax.axis_size("wide") * lax.axis_size("narrow")
    experts = devices // 2
    capacity = 2 * tok_rows * top_count // experts
    half_width = model_width // 2
    expert_ids = routes.reshape(-1)
    slot_index = slot_numbers(expert_ids, experts)
    source = jnp.repeat(jnp.arange(tok_rows, dtype=jnp.int32), top_count)
    weighted = (gates.reshape(-1)[:, None] * cotangent[source].astype(jnp.float32)).astype(
        jnp.bfloat16
    )
    zero_buffer = jnp.zeros((experts, capacity, model_width), jnp.bfloat16)
    x_buffer = zero_buffer.at[expert_ids, slot_index].set(hidden[source])
    dy_buffer = zero_buffer.at[expert_ids, slot_index].set(weighted)
    parity = lax.axis_index("narrow") % 2
    x_sent = jnp.repeat(x_buffer, 2, axis=0)
    dy_sent = jnp.repeat(dy_buffer, 2, axis=0)
    x_rows, dy_rows = (
        lax.all_to_all(x_sent, ("wide", "narrow"), split_axis=0, concat_axis=0, tiled=True),
        lax.all_to_all(dy_sent, ("wide", "narrow"), split_axis=0, concat_axis=0, tiled=True),
    )
    x_rows = x_rows.reshape(devices * capacity, model_width)
    dy_rows = dy_rows.reshape(devices * capacity, model_width)
    gate_local = w_gate[0]
    up_local = w_up[0]
    down_local = w_down[0]
    contract_last = (((1,), (1,)), ((), ()))
    pre_gate = jnp.dot(x_rows, gate_local, preferred_element_type=jnp.float32)
    up_value = jnp.dot(x_rows, up_local, preferred_element_type=jnp.float32)
    grad_hidden = lax.dot_general(
        dy_rows, down_local, contract_last, preferred_element_type=jnp.float32
    )
    sigmoid_gate = jax.nn.sigmoid(pre_gate)
    grad_gate = (
        grad_hidden * up_value * sigmoid_gate * (1.0 + pre_gate * (1.0 - sigmoid_gate))
    ).astype(jnp.bfloat16)
    grad_up = (grad_hidden * pre_gate * sigmoid_gate).astype(jnp.bfloat16)
    partial_grad = lax.dot_general(
        grad_gate, gate_local, contract_last, preferred_element_type=jnp.float32
    )
    partial_grad = partial_grad + lax.dot_general(
        grad_up, up_local, contract_last, preferred_element_type=jnp.float32
    )
    own_part = lax.dynamic_slice_in_dim(partial_grad, parity * half_width, half_width, 1)
    peer_part = lax.dynamic_slice_in_dim(partial_grad, (1 - parity) * half_width, half_width, 1)
    summed = (own_part + swapped(peer_part, "narrow", 0)).astype(jnp.bfloat16)
    returned = lax.all_to_all(
        summed.reshape(devices, capacity, half_width),
        ("wide", "narrow"),
        split_axis=0,
        concat_axis=0,
        tiled=True,
    )
    returned = (
        returned.reshape(experts, 2, capacity, half_width)
        .transpose(0, 2, 1, 3)
        .reshape(experts, capacity, model_width)
    )
    routed = (
        returned[expert_ids, slot_index]
        .astype(jnp.float32)
        .reshape(tok_rows, top_count, model_width)
        .sum(axis=1)
    )
    resid_grad = (cotangent.astype(jnp.float32) + routed).astype(jnp.bfloat16)
    tok_wide = q_nope.shape[0]
    heads_local = q_nope.shape[1] // NOPE
    score_scale = 1.0 / math.sqrt(NOPE + ROPE)
    grad_out = lax.dot_general(
        lax.all_gather(resid_grad, "narrow", axis=0, tiled=True),
        w_out,
        contract_last,
        preferred_element_type=jnp.float32,
    ).astype(jnp.bfloat16)
    latent_all, rope_all = (
        lax.all_gather(latent, "wide", axis=0, tiled=True),
        lax.all_gather(rope_key, "wide", axis=0, tiled=True),
    )
    wide_index = lax.axis_index("wide")
    local_steps = jnp.arange(tok_wide, dtype=jnp.int32)
    query_pos = offsets[wide_index] * tok_wide + local_steps
    key_pos = (offsets[:, None] * tok_wide + local_steps[None, :]).reshape(-1)
    visible = key_pos[None, :] <= query_pos[:, None]
    q_heads = q_nope.reshape(tok_wide, heads_local, NOPE)
    pe_heads = q_pe.reshape(tok_wide, heads_local, ROPE)
    uk_heads = w_uk.reshape(heads_local, NOPE, LATENT)
    uv_heads = w_uv.reshape(heads_local, VDIM, LATENT)
    query_latent = jnp.einsum(
        "thn,hnl->htl", q_heads, uk_heads, preferred_element_type=jnp.float32
    ).astype(jnp.bfloat16)
    out_latent = jnp.einsum(
        "thv,hvl->htl",
        grad_out.reshape(tok_wide, heads_local, VDIM),
        uv_heads,
        preferred_element_type=jnp.float32,
    ).astype(jnp.bfloat16)
    scores = score_scale * (
        jnp.einsum("htl,sl->hts", query_latent, latent_all, preferred_element_type=jnp.float32)
        + jnp.einsum("thr,sr->hts", pe_heads, rope_all, preferred_element_type=jnp.float32)
    )
    masked = jnp.where(visible[None, :, :], scores, -1e30)
    row_max = jnp.max(masked, axis=2, keepdims=True)
    log_norm = row_max + jnp.log(jnp.sum(jnp.exp(masked - row_max), axis=2, keepdims=True))
    probs = jnp.exp(masked - log_norm)
    grad_probs = jnp.einsum(
        "htl,sl->hts", out_latent, latent_all, preferred_element_type=jnp.float32
    )
    row_delta = jnp.sum(probs * grad_probs, axis=2, keepdims=True)
    grad_scores = (score_scale * probs * (grad_probs - row_delta)).astype(jnp.bfloat16)
    probs_low = probs.astype(jnp.bfloat16)
    grad_qlat = jnp.einsum(
        "hts,sl->htl", grad_scores, latent_all, preferred_element_type=jnp.float32
    ).astype(jnp.bfloat16)
    grad_q_nope = jnp.einsum(
        "htl,hnl->thn", grad_qlat, uk_heads, preferred_element_type=jnp.float32
    )
    grad_q_nope = grad_q_nope.astype(jnp.bfloat16).reshape(tok_wide, heads_local * NOPE)
    grad_q_pe = jnp.einsum("hts,sr->thr", grad_scores, rope_all, preferred_element_type=jnp.float32)
    grad_q_pe = grad_q_pe.astype(jnp.bfloat16).reshape(tok_wide, heads_local * ROPE)
    latent_term = jnp.einsum(
        "hts,htl->sl", probs_low, out_latent, preferred_element_type=jnp.float32
    )
    latent_term = latent_term + jnp.einsum(
        "hts,htl->sl", grad_scores, query_latent, preferred_element_type=jnp.float32
    )
    rope_term = jnp.einsum("hts,thr->sr", grad_scores, pe_heads, preferred_element_type=jnp.float32)
    block_latent, block_rope = jax.tree.map(
        lambda part: lax.psum_scatter(
            part.astype(jnp.bfloat16), "wide", scatter_dimension=0, tiled=True
        ).astype(jnp.float32),
        (latent_term, rope_term),
    )
    grad_latent, grad_rope_key = (
        lax.psum_scatter(
            block_latent.astype(jnp.bfloat16), "narrow", scatter_dimension=0, tiled=True
        ).astype(jnp.float32),
        lax.psum_scatter(
            block_rope.astype(jnp.bfloat16), "narrow", scatter_dimension=0, tiled=True
        ).astype(jnp.float32),
    )
    return (resid_grad, grad_q_nope, grad_q_pe, grad_latent, grad_rope_key)


def solution(mesh):
    return jax.shard_map(
        on_device,
        mesh=mesh,
        in_specs=(
            P(("wide", "narrow"), None),
            P(("wide", "narrow"), None),
            P(("wide", "narrow"), None),
            P(("wide", "narrow"), None),
            P(),
            P(("wide", "narrow"), None, None),
            P(("wide", "narrow"), None, None),
            P(("wide", "narrow"), None, None),
            P("narrow", None),
            P("wide", None),
            P("wide", None),
            P("wide", "narrow"),
            P("wide", "narrow"),
            P("narrow", None),
            P("narrow", None),
        ),
        out_specs=(
            P(("wide", "narrow"), None),
            P("wide", "narrow"),
            P("wide", "narrow"),
            P(("wide", "narrow"), None),
            P(("wide", "narrow"), None),
        ),
        check_vma=False,
    )
```

profile of v0, /device:TPU:0, one launch (start us, length us, event | category | flops | bytes accessed | tf_op | source)
XLA Modules:
  0.0 863.9 jit_solution(11751206266569349338)
XLA Ops:
  15.2 70.4 %scatter_fusion.1 = bf16[16,48,2048]{2,1,0:T(8,128)(2,1)} fusion(bf16[16,48,2048]{2,1,0:T(8,128)(2,1)} %broadcast_in_dim.18.clone, s32[384]{0:T(512)S(1)} %get-tuple-element.21, bf16[384,2048]{1,0:T(8,128)(2,1)} %gather_fusion.1), kind=kCustom, calls=%fused_computation.4 | custom fusion | bytes 4721664 | tf_op jit(solution)/shard_map/scatter | solution.py:58
  85.7 5.5 broadcast_in_dim.25
  91.2 7.3 all-to-all-start.1
  106.7 70.5 %scatter_fusion = bf16[16,48,2048]{2,1,0:T(8,128)(2,1)} fusion(bf16[16,48,2048]{2,1,0:T(8,128)(2,1)} %broadcast_in_dim.18.clone.1, s32[384]{0:T(512)S(1)} %get-tuple-element.21, bf16[384,2048]{1,0:T(8,128)(2,1)} %multiply_convert_fusion.3), kind=kCustom, calls=%fused_computation.3 | custom fusion | bytes 4721664 | tf_op jit(solution)/shard_map/scatter | solution.py:59
  177.2 58.1 %all-to-all-done.1 = bf16[32,48,2048]{2,1,0:T(8,128)(2,1)} async-done(((bf16[32,48,2048]{2,1,0:T(8,128)(2,1)}), bf16[32,48,2048]{2,1,0:T(8,128)(2,1)}, u32[]{:S(2)}, u32[]{:S(2)}) %all-to-all-start.1) | async-done | bytes 6291488 | tf_op jit(solution)/shard_map/all_to_all | solution.py:64
  235.3 5.5 broadcast_in_dim.20
  240.8 7.4 all-to-all-start
  248.2 10.4 %fusion.9 = f32[1536,704]{0,1:T(8,128)} fusion(bf16[1536,2048]{1,0:T(8,128)(2,1)} %bitcast.5, bf16[1,2048,704]{1,2,0:T(8,128)(2,1)} %param.20), kind=kOutput, calls=%fused_computation.26 | convolution fusion | flops 4429185024 | bytes 13500416 | tf_op jit(solution)/shard_map/dot_general | solution.py:73
  258.6 126.5 %all-to-all-done = bf16[32,48,2048]{2,1,0:T(8,128)(2,1)} async-done(((bf16[32,48,2048]{2,1,0:T(8,128)(2,1)}), bf16[32,48,2048]{2,1,0:T(8,128)(2,1)}, u32[]{:S(2)}, u32[]{:S(2)}) %all-to-all-start) | async-done | bytes 6291488 | tf_op jit(solution)/shard_map/all_to_all | solution.py:65
  385.1 10.4 %fusion.15 = f32[1536,704]{0,1:T(8,128)} fusion(bf16[1536,2048]{1,0:T(8,128)(2,1)} %bitcast.2, bf16[1,704,2048]{2,1,0:T(8,128)(2,1)} %param.22), kind=kOutput, calls=%fused_computation.30 | convolution fusion | flops 4429185024 | bytes 13500416 | tf_op jit(solution)/shard_map/dot_general | solution.py:75
  395.5 21.0 %fusion.7 = f32[1536,2048]{1,0:T(8,128)} fusion(bf16[1,2048,704]{1,2,0:T(8,128)(2,1)} %param.20, f32[1536,704]{0,1:T(8,128)} %fusion.9, f32[1536,704]{0,1:T(8,128)} %fusion.15, bf16[1536,2048]{1,0:T(8,128)(2,1)} %bitcast.5, bf16[1,2048,704]{1,2,0:T(8,128)(2,1)S(1)} %copy-done), kind=kOutput, calls=%fused_computation.24 | convolution fusion | flops 8869183488 | bytes 33292288 | tf_op jit(solution)/shard_map/dot_general | solution.py:83
  416.4 11.2 %convolution_add_fusion = f32[1536,2048]{1,0:T(8,128)S(1)} fusion(f32[1536,2048]{1,0:T(8,128)} %fusion.7, bf16[1,2048,704]{1,2,0:T(8,128)(2,1)S(1)} %copy-done, f32[1536,704]{0,1:T(8,128)} %fusion.15, f32[1536,704]{0,1:T(8,128)} %fusion.9), kind=kOutput, calls=%fused_computation.5 | convolution fusion | flops 4438818816 | bytes 36700160 | tf_op jit(solution)/shard_map/dot_general | solution.py:86
  434.2 4.1 collective-permute-start
  438.2 136.4 %collective-permute-done = f32[1536,1024]{1,0:T(8,128)} collective-permute-done((f32[1536,1024]{1,0:T(8,128)}, f32[1536,1024]{1,0:T(8,128)}, u32[]{:S(2)}, u32[]{:S(2)}) %collective-permute-start) | collective-permute-done | bytes 6291488 | tf_op jit(solution)/shard_map/ppermute | solution.py:17
  574.6 7.4 add_convert_fusion
  582.0 3.7 all-to-all-start.2
  588.0 27.6 %all_gather.10 = bf16[2048,64]{0,1:T(8,128)(2,1)S(1)} all-gather(bf16[256,64]{0,1:T(8,128)(2,1)S(1)} %copy-done.14), channel_id=1, replica_groups=mesh['wide'=8,'narrow'=4] {'wide'}, dimensions={0}, use_global_device_ids=true | all-gather | bytes 294912 | tf_op jit(solution)/shard_map/all_gather | solution.py:122
  617.4 38.3 %all-to-all-done.2 = bf16[32,48,1024]{2,1,0:T(8,128)(2,1)} async-done(((bf16[32,48,1024]{2,1,0:T(8,128)(2,1)}), bf16[32,48,1024]{2,1,0:T(8,128)(2,1)}, u32[]{:S(2)}, u32[]{:S(2)}) %all-to-all-start.2) | async-done | bytes 3145760 | tf_op jit(solution)/shard_map/all_to_all | solution.py:92
  655.6 6.8 copy.80
  662.5 6.1 reshape.219
  668.6 12.0 %gather_fusion.2 = bf16[384,2048]{1,0:T(8,128)(2,1)S(1)} fusion(bf16[16,48,2048]{2,1,0:T(8,128)(2,1)} %reshape.219, s32[384]{0:T(512)S(1)} %get-tuple-element.20), kind=kCustom, calls=%fused_computation.2 | custom fusion | bytes 3148800 | tf_op jit(solution)/shard_map/gather | solution.py:105
  682.8 3.6 reduce_sum.40
  687.5 4.0 fusion.24
  697.3 18.1 %all-gather.5.cloned.1.call-done = bf16[256,2048]{1,0:T(8,128)(2,1)} async-done(((bf16[64,2048]{1,0:T(8,128)(2,1)}), bf16[256,2048]{1,0:T(8,128)(2,1)}) %all-gather.5.cloned.1.call-update) | async-done | bytes 1048592 | tf_op jit(solution)/shard_map/all_gather | solution.py:115
  718.5 8.2 fusion.3
  735.6 7.2 fusion.5
  742.9 25.8 %reduce-scatter.11.cloned.1.call-done = bf16[256,64]{0,1:T(8,128)(2,1)} async-done(((bf16[2048,64]{0,1:T(8,128)(2,1)}), bf16[256,64]{0,1:T(8,128)(2,1)}) %reduce-scatter.11.cloned.1.call-update) | async-done | bytes 32784 | tf_op jit(solution)/shard_map/reduce_scatter | solution.py:173
  770.3 43.2 %reduce-scatter.7.cloned.1.call-done = bf16[256,512]{1,0:T(8,128)(2,1)} async-done(((bf16[2048,512]{1,0:T(8,128)(2,1)}), bf16[256,512]{1,0:T(8,128)(2,1)}) %reduce-scatter.7.cloned.1.call-update) | async-done | bytes 262160 | tf_op jit(solution)/shard_map/reduce_scatter | solution.py:173
  813.5 5.6 fusion.32
  820.0 3.6 convolution_convert_fusion.3
  824.3 10.9 %reduce-scatter.13.cloned.1.call-done = bf16[64,64]{1,0:T(8,128)(2,1)} async-done(((bf16[256,64]{1,0:T(8,128)(2,1)}), bf16[64,64]{1,0:T(8,128)(2,1)}) %reduce-scatter.13.cloned.1.call-update) | async-done | bytes 8208
  836.7 18.5 %reduce-scatter.9.cloned.1.call-done = bf16[64,512]{1,0:T(8,128)(2,1)} async-done(((bf16[256,512]{1,0:T(8,128)(2,1)}), bf16[64,512]{1,0:T(8,128)(2,1)}) %reduce-scatter.9.cloned.1.call-update) | async-done | bytes 65552 | tf_op jit(solution)/shard_map/reduce_scatter | solution.py:179
  (98 shorter events, 53.3 us)
Async XLA Ops:
  7.2 388.3 %copy-start = (bf16[1,2048,704]{1,2,0:T(8,128)(2,1)S(1)}, bf16[1,2048,704]{1,2,0:T(8,128)(2,1)}, u32[]{:S(2)}) copy-start(bf16[1,2048,704]{1,2,0:T(8,128)(2,1)} %param.21) | copy-start | bytes 8650756
  7.2 2.8 copy-start.3
  91.2 7.3 copy-start.2
  91.2 144.2 %all-to-all-start.1 = ((bf16[32,48,2048]{2,1,0:T(8,128)(2,1)}), bf16[32,48,2048]{2,1,0:T(8,128)(2,1)}, u32[]{:S(2)}, u32[]{:S(2)}) async-start(bf16[32,48,2048]{2,1,0:T(8,128)(2,1)} %bitcast.129), calls=%async_computation.1 | async-start | bytes 12582912 | tf_op jit(solution)/shard_map/all_to_all | solution.py:64
  98.4 3.1 copy-start.15
  240.8 144.3 %all-to-all-start = ((bf16[32,48,2048]{2,1,0:T(8,128)(2,1)}), bf16[32,48,2048]{2,1,0:T(8,128)(2,1)}, u32[]{:S(2)}, u32[]{:S(2)}) async-start(bf16[32,48,2048]{2,1,0:T(8,128)(2,1)} %bitcast.128), calls=%async_computation | async-start | bytes 12582912 | tf_op jit(solution)/shard_map/all_to_all | solution.py:65
  427.7 6.5 copy-start.6
  434.2 140.4 %collective-permute-start = (f32[1536,1024]{1,0:T(8,128)}, f32[1536,1024]{1,0:T(8,128)}, u32[]{:S(2)}, u32[]{:S(2)}) collective-permute-start(f32[1536,1024]{1,0:T(8,128)} %constant_dynamic-slice_fusion), channel_id=1, source_target_pairs={{0,1},{1,0},{2,3},{3,2},{4,5},{5,4},{6,7},{7,6},{8,9},{9,8},{10,11... | collective-permute-start | bytes 18874376 | tf_op jit(solution)/shard_map/ppermute | solution.py:17
  582.0 4.5 copy-start.13
  582.0 4.6 copy-start.16
  582.0 6.0 copy-start.14
  582.0 33.6 %copy-start.11 = (bf16[512,512]{1,0:T(8,128)(2,1)S(1)}, bf16[512,512]{1,0:T(8,128)(2,1)}, u32[]{:S(2)}) copy-start(bf16[512,512]{1,0:T(8,128)(2,1)} %param.28) | copy-start | bytes 1572868
  582.0 33.6 %copy-start.12 = (bf16[256,512]{1,0:T(8,128)(2,1)S(1)}, bf16[256,512]{1,0:T(8,128)(2,1)}, u32[]{:S(2)}) copy-start(bf16[256,512]{1,0:T(8,128)(2,1)} %param.26) | copy-start | bytes 786436
  582.0 73.6 %all-to-all-start.2 = ((bf16[32,48,1024]{2,1,0:T(8,128)(2,1)}), bf16[32,48,1024]{2,1,0:T(8,128)(2,1)}, u32[]{:S(2)}, u32[]{:S(2)}) async-start(bf16[32,48,1024]{2,1,0:T(8,128)(2,1)} %bitcast.131), calls=%async_computation.2 | async-start | bytes 6291456 | tf_op jit(solution)/shard_map/all_to_all | solution.py:92
  585.7 101.7 %all-gather.3.cloned.1.call-start = ((), (), s32[]{:S(2)}) async-start(), calls=%async_computation.7 | async-start | bytes 2359296 | tf_op jit(solution)/shard_map/all_gather | solution.py:121
  586.5 128.9 %all-gather.5.cloned.1.call-start = ((), (), s32[]{:S(2)}) async-start(), calls=%async_computation.8 | async-start | bytes 1310720 | tf_op jit(solution)/shard_map/all_gather | solution.py:115
  682.8 4.7 copy-start.8
  687.2 81.6 %reduce-scatter.11.cloned.1.call-start = ((), (), s32[]{:S(2)}) async-start(), calls=%async_computation.11 | async-start | bytes 294912 | tf_op jit(solution)/shard_map/reduce_scatter | solution.py:173
  694.0 3.2 copy-start.4
  694.0 24.0 %copy-start.10 = (bf16[512,512]{1,0:T(8,128)(2,1)S(1)}, bf16[512,512]{1,0:T(8,128)(2,1)}, u32[]{:S(2)}) copy-start(bf16[512,512]{1,0:T(8,128)(2,1)} %param.29) | copy-start | bytes 1572868
  718.1 8.6 %slice-start = ((s8[8388608]{0:T(1024)(128)(4,1)}), s8[4194304]{0:T(1024)(128)(4,1)S(1)}, s32[]{:S(2)}) async-start(s8[8388608]{0:T(1024)(128)(4,1)} %bitcast.126), calls=%async_computation.13 | async-start | bytes 8388608
  718.5 8.2 slice-start.1
  718.5 8.2 copy-start.7
  731.8 1.9 copy-start.5
  733.8 1.9 copy-start.9
  735.3 78.1 %reduce-scatter.7.cloned.1.call-start = ((), (), s32[]{:S(2)}) async-start(), calls=%async_computation.9 | async-start | bytes 2359296 | tf_op jit(solution)/shard_map/reduce_scatter | solution.py:173
  742.9 92.4 %reduce-scatter.13.cloned.1.call-start = ((), (), s32[]{:S(2)}) async-start(), calls=%async_computation.12 | async-start | bytes 81920
  770.2 85.0 %reduce-scatter.9.cloned.1.call-start = ((), (), s32[]{:S(2)}) async-start(), calls=%async_computation.10 | async-start | bytes 327680 | tf_op jit(solution)/shard_map/reduce_scatter | solution.py:179
  813.5 43.2 %copy-start.1 = (bf16[1,2048,704]{1,2,0:T(8,128)(2,1)S(1)}, bf16[1,2048,704]{1,2,0:T(8,128)(2,1)}, u32[]{:S(2)}) copy-start(bf16[1,2048,704]{1,2,0:T(8,128)(2,1)} %param.21) | copy-start | bytes 8650756
Sparse Core Ops, SparseCore 0:
  588.4 44.8 all-gather.2
  687.3 28.0 all-gather.4
  735.5 33.2 reduce-scatter.10
  772.2 41.2 reduce-scatter.6
  816.1 19.0 reduce-scatter.12
  837.4 17.7 reduce-scatter.8
where the time goes:
time: 873 us; the launch traced here: 864 us
  waiting for transfers between devices  477 us (55%)
  local copies, waits for them, and re-layouts  207 us (24%)
  matrix products  93.1 us (11%)
  blocking collectives  27.6 us (3%)
  starting transfers between devices  23.1 us (3%)
  other arithmetic  21 us (2%)
  between operations  15.4 us (2%)
    ppermute x1, waiting for transfers between devices, swapped(): return lax.ppermute(value, axis, pairs)  136 us
    all_to_all x1, waiting for transfers between devices, on_device(): lax.all_to_all(dy_sent, ('wide', 'narrow'), split_axis=0, concat_axis=0,...  127 us
    scatter x1, local copies, waits for them, and re-layouts, on_device(): dy_buffer = zero_buffer.at[expert_ids, slot_index].set(weighted)  70.5 us
    scatter x1, local copies, waits for them, and re-layouts, on_device(): x_buffer = zero_buffer.at[expert_ids, slot_index].set(hidden[source])  70.4 us
    reduce_scatter x2, waiting for transfers between devices, on_device(): lax.psum_scatter(part.astype(jnp.bfloat16), 'wide', scatter_dimension=0,...  69 us
    all_to_all x1, waiting for transfers between devices, on_device(): lax.all_to_all(x_sent, ('wide', 'narrow'), split_axis=0, concat_axis=0, t...  58.1 us
    all_to_all x1, waiting for transfers between devices, on_device(): lax.all_to_all(summed.reshape(devices, capacity, half_width), ('wide', 'n...  38.3 us
    all_gather x1, blocking collectives, on_device(): lax.all_gather(rope_key, 'wide', axis=0, tiled=True)  27.6 us
  transfers between devices with their start and end apart: 10, of which 9 were waited for; matrix products, arithmetic and copies ran while one was open for 18% of the time, Pallas kernels for 0%

commit v1 on v0

--- a/solution.py
+++ b/solution.py
@@ -1,8 +1,11 @@
+import functools
 import math
 
 import jax
 import jax.numpy as jnp
 from jax import lax
+from jax.experimental import pallas as pl
+from jax.experimental.pallas import tpu as pltpu
 from jax.sharding import PartitionSpec as P
 
 LATENT = 512
@@ -10,19 +13,168 @@
 ROPE = 64
 VDIM = 128
 
-
-def swapped(value, axis, distance):
-    mask = 2**distance
-    pairs = [(source, source ^ mask) for source in range(lax.axis_size(axis))]
-    return lax.ppermute(value, axis, pairs)
-
-
-def slot_numbers(expert_ids, experts):
-    onehot = (expert_ids[:, None] == jnp.arange(experts, dtype=jnp.int32)[None, :]).astype(
-        jnp.int32
-    )
-    before = jnp.cumsum(onehot, axis=0) - onehot
-    return jnp.sum(before * onehot, axis=1)
+F32 = jnp.float32
+BF16 = jnp.bfloat16
+CONTRACT_LAST = (((1,), (1,)), ((), ()))
+
+
+def across(value, mask):
+    pairs = [(source, source ^ mask) for source in range(lax.axis_size("wide"))]
+    return lax.ppermute(value, "wide", pairs)
+
+
+def along(value):
+    size = lax.axis_size("narrow")
+    return lax.ppermute(value, "narrow", [(i, (i + 1) % size) for i in range(size)])
+
+
+def wide_levels():
+    size = lax.axis_size("wide")
+    masks = []
+    mask = size // 2
+    while mask:
+        masks.append(mask)
+        mask //= 2
+    first, rest = masks[:2], masks[2:]
+    return first, [rest[i : i + 2] for i in range(0, len(rest), 2)]
+
+
+def gather_level(block, level):
+    if len(level) == 1:
+        return [block, across(block, level[0])]
+    high, low = level
+    by_low, by_high = across(block, low), across(block, high)
+    half = block.shape[0] // 2
+    corner = jnp.concatenate([across(by_low[:half], high), across(by_high[half:], low)], axis=0)
+    return [block, by_low, by_high, corner]
+
+
+def total(*terms):
+    summed = terms[0].astype(F32)
+    for term in terms[1:]:
+        summed = summed + term.astype(F32)
+    return summed.astype(BF16)
+
+
+def scatter_level(blocks, level):
+    if len(level) == 1:
+        return total(blocks[0], across(blocks[1], level[0]))
+    high, low = level
+    own, by_low, by_high, corner = blocks
+    half = own.shape[1] // 2
+    from_high = across(corner[:, :half], high)
+    from_low = across(corner[:, half:], low)
+    by_low = jnp.concatenate([total(by_low[:, :half], from_high), by_low[:, half:]], axis=1)
+    by_high = jnp.concatenate([by_high[:, :half], total(by_high[:, half:], from_low)], axis=1)
+    return total(own, across(by_low, low), across(by_high, high))
+
+
+def expert_kernel(count, gate_ref, *refs):
+    tokens, (w_gate, w_up, w_down), outs = refs[:count], refs[count : count + 3], refs[count + 3 :]
+    for index in range(count):
+        pieces, _, rows, width = tokens[index].shape
+        merged = pieces * rows
+        x_rows = tokens[index][:, 0].reshape(merged, width)
+        dy_rows = tokens[index][:, 1].reshape(merged, width)
+        gate = gate_ref[pl.ds(index * merged, merged), :]
+        pre_gate = jnp.dot(x_rows, w_gate[...], preferred_element_type=F32)
+        up_value = jnp.dot(x_rows, w_up[...], preferred_element_type=F32)
+        grad_hidden = gate * lax.dot_general(
+            dy_rows, w_down[...], CONTRACT_LAST, preferred_element_type=F32
+        )
+        sigmoid_gate = jax.nn.sigmoid(pre_gate)
+        grad_gate = grad_hidden * up_value * sigmoid_gate * (1.0 + pre_gate * (1.0 - sigmoid_gate))
+        grad_up = grad_hidden * pre_gate * sigmoid_gate
+        partial_grad = lax.dot_general(
+            grad_gate.astype(BF16), w_gate[...], CONTRACT_LAST, preferred_element_type=F32
+        )
+        partial_grad = partial_grad + lax.dot_general(
+            grad_up.astype(BF16), w_up[...], CONTRACT_LAST, preferred_element_type=F32
+        )
+        outs[index][...] = partial_grad.astype(BF16)
+
+
+def expert_grads(tokens, gate, w_gate, w_up, w_down):
+    count = len(tokens)
+    pieces, _, rows, width = tokens[0].shape
+    merged = pieces * rows
+    flops = 2 * 5 * count * merged * width * w_gate.shape[1]
+    return pl.pallas_call(
+        functools.partial(expert_kernel, count),
+        out_shape=[jax.ShapeDtypeStruct((merged, width), BF16)] * count,
+        in_specs=[pl.BlockSpec(memory_space=pltpu.VMEM)] * (count + 4),
+        out_specs=[pl.BlockSpec(memory_space=pltpu.VMEM)] * count,
+        compiler_params=pltpu.CompilerParams(vmem_limit_bytes=40 * 2**20),
+        cost_estimate=pl.CostEstimate(
+            flops=flops, bytes_accessed=3 * w_gate.size * 2 + 6 * count * merged * width, transcendentals=0
+        ),
+    )(gate, *tokens, w_gate, w_up, w_down)
+
+
+def routed_sum(hidden, cotangent, routes, gates, w_gate, w_up, w_down):
+    rows, width = hidden.shape
+    wide_size, ring = lax.axis_size("wide"), lax.axis_size("narrow")
+    wide_index, ring_index = lax.axis_index("wide"), lax.axis_index("narrow")
+    experts = wide_size * ring // 2
+    expert = (wide_index * ring + ring_index) // 2
+    named = routes[:, :, None] == jnp.arange(experts, dtype=jnp.int32)[None, None, :]
+    dense = jnp.sum(jnp.where(named, gates[:, :, None], 0.0), axis=1)
+    dense_all = lax.all_gather(dense, ("wide", "narrow"), axis=0, tiled=True)
+    column = lax.dynamic_slice_in_dim(dense_all, expert, 1, 1).reshape(wide_size, ring, rows)
+
+    (high, low), rest = wide_levels()
+    corner_mask = high | low
+    order = [0, low, high, corner_mask]
+    for level in rest:
+        extra = [0, level[0]] if len(level) == 1 else [0, level[1], level[0], level[0] | level[1]]
+        order = [mask ^ more for more in extra for mask in order]
+    places = wide_index ^ jnp.array(order, jnp.int32)
+
+    own = jnp.concatenate([hidden, cotangent], axis=0)
+    corner = None
+    link_own = link_corner = None
+    home = None
+    for step in range(ring):
+        if step:
+            own = along(own)
+        by_low, by_high = across(own, low), across(own, high)
+        in_plane = step == 0 or step == ring - 1
+        if in_plane:
+            corner = jnp.concatenate(
+                [across(by_low[:rows], high), across(by_high[rows:], low)], axis=0
+            )
+        else:
+            corner = along(corner)
+        blocks = [jnp.concatenate([own, by_low, by_high, corner], axis=0)]
+        for level in rest:
+            blocks = [piece for block in zip(*[gather_level(b, level) for b in blocks]) for piece in block]
+        tokens = [block.reshape(4, 2, rows, width) for block in blocks]
+        source = (ring_index - step) % ring
+        gate = lax.dynamic_index_in_dim(column, source, 1, False)[places].reshape(-1, 1)
+        partials = expert_grads(tokens, gate, w_gate, w_up, w_down)
+        for level in reversed(rest):
+            size = 2 ** len(level)
+            group = len(partials) // size
+            partials = [
+                scatter_level([partials[i + group * j] for j in range(size)], level)
+                for i in range(group)
+            ]
+        piece_own, piece_low, piece_high, piece_corner = partials[0].reshape(4, rows, width)
+        if link_corner is not None:
+            piece_corner = total(piece_corner, along(link_corner))
+        if in_plane:
+            summed = scatter_level([piece_own, piece_low, piece_high, piece_corner], (high, low))
+            link_corner = None
+        else:
+            summed = total(piece_own, across(piece_low, low), across(piece_high, high))
+            link_corner = piece_corner
+        if step == 0:
+            home = summed
+        elif link_own is None:
+            link_own = summed
+        else:
+            link_own = total(summed, along(link_own))
+    return home.astype(F32) + along(link_own).astype(F32)
 
 
 def on_device(
@@ -42,72 +194,9 @@
     w_uk,
     w_uv,
 ):
-    tok_rows, model_width = hidden.shape
-    top_count = routes.shape[1]
-    devices = lax.axis_size("wide") * lax.axis_size("narrow")
-    experts = devices // 2
-    capacity = 2 * tok_rows * top_count // experts
-    half_width = model_width // 2
-    expert_ids = routes.reshape(-1)
-    slot_index = slot_numbers(expert_ids, experts)
-    source = jnp.repeat(jnp.arange(tok_rows, dtype=jnp.int32), top_count)
-    weighted = (gates.reshape(-1)[:, None] * cotangent[source].astype(jnp.float32)).astype(
-        jnp.bfloat16
-    )
-    zero_buffer = jnp.zeros((experts, capacity, model_width), jnp.bfloat16)
-    x_buffer = zero_buffer.at[expert_ids, slot_index].set(hidden[source])
-    dy_buffer = zero_buffer.at[expert_ids, slot_index].set(weighted)
-    parity = lax.axis_index("narrow") % 2
-    x_sent = jnp.repeat(x_buffer, 2, axis=0)
-    dy_sent = jnp.repeat(dy_buffer, 2, axis=0)
-    x_rows, dy_rows = (
-        lax.all_to_all(x_sent, ("wide", "narrow"), split_axis=0, concat_axis=0, tiled=True),
-        lax.all_to_all(dy_sent, ("wide", "narrow"), split_axis=0, concat_axis=0, tiled=True),
-    )
-    x_rows = x_rows.reshape(devices * capacity, model_width)
-    dy_rows = dy_rows.reshape(devices * capacity, model_width)
-    gate_local = w_gate[0]
-    up_local = w_up[0]
-    down_local = w_down[0]
-    contract_last = (((1,), (1,)), ((), ()))
-    pre_gate = jnp.dot(x_rows, gate_local, preferred_element_type=jnp.float32)
-    up_value = jnp.dot(x_rows, up_local, preferred_element_type=jnp.float32)
-    grad_hidden = lax.dot_general(
-        dy_rows, down_local, contract_last, preferred_element_type=jnp.float32
-    )
-    sigmoid_gate = jax.nn.sigmoid(pre_gate)
-    grad_gate = (
-        grad_hidden * up_value * sigmoid_gate * (1.0 + pre_gate * (1.0 - sigmoid_gate))
-    ).astype(jnp.bfloat16)
-    grad_up = (grad_hidden * pre_gate * sigmoid_gate).astype(jnp.bfloat16)
-    partial_grad = lax.dot_general(
-        grad_gate, gate_local, contract_last, preferred_element_type=jnp.float32
-    )
-    partial_grad = partial_grad + lax.dot_general(
-        grad_up, up_local, contract_last, preferred_element_type=jnp.float32
-    )
-    own_part = lax.dynamic_slice_in_dim(partial_grad, parity * half_width, half_width, 1)
-    peer_part = lax.dynamic_slice_in_dim(partial_grad, (1 - parity) * half_width, half_width, 1)
-    summed = (own_part + swapped(peer_part, "narrow", 0)).astype(jnp.bfloat16)
-    returned = lax.all_to_all(
-        summed.reshape(devices, capacity, half_width),
-        ("wide", "narrow"),
-        split_axis=0,
-        concat_axis=0,
-        tiled=True,
-    )
-    returned = (
-        returned.reshape(experts, 2, capacity, half_width)
-        .transpose(0, 2, 1, 3)
-        .reshape(experts, capacity, model_width)
-    )
-    routed = (
-        returned[expert_ids, slot_index]
-        .astype(jnp.float32)
-        .reshape(tok_rows, top_count, model_width)
-        .sum(axis=1)
-    )
+    routed = routed_sum(hidden, cotangent, routes, gates, w_gate[0], w_up[0], w_down[0])
     resid_grad = (cotangent.astype(jnp.float32) + routed).astype(jnp.bfloat16)
+    contract_last = CONTRACT_LAST
     tok_wide = q_nope.shape[0]
     heads_local = q_nope.shape[1] // NOPE
     score_scale = 1.0 / math.sqrt(NOPE + ROPE)

time: 873 us -> 468 us (0.54)
  waiting for transfers between devices: 477 us -> 178 us
  local copies, waits for them, and re-layouts: 207 us -> 44.1 us
  blocking collectives: 27.6 us -> 83 us
  matrix products: 93.1 us -> 39.8 us
  Pallas kernels: 0 us -> 50.4 us
  starting transfers between devices: 23.1 us -> 37 us
    all_to_all x3 -> x0, waiting for transfers between devices: 223 us -> none  [the longest x1 127 us: on_device(): lax.all_to_all(dy_sent, ('wide', 'narrow'), split_axis=0, concat_axis=0,...]
    scatter x2 -> x0, local copies, waits for them, and re-layouts: 141 us -> none  [the longest x1 70.5 us: on_device(): dy_buffer = zero_buffer.at[expert_ids, slot_index].set(weighted)]
    ppermute x1 -> x42, waiting for transfers between devices: 136 us -> 63.8 us  [the longest x10 48.7 us: along(): lax.ppermute(value, 'narrow', [(i, (i + 1) % size) for i in range(size)])]
    all_gather x0 -> x1, blocking collectives: none -> 71.6 us  [routed_sum(): dense_all = lax.all_gather(dense, ('wide', 'narrow'), axis=0, tiled=True)]
    dot_general x4 -> x0, matrix products: 52.9 us -> none  [the longest x1 21 us: on_device(): lax.dot_general(grad_gate, gate_local, contract_last, preferred_element_t...]
    pallas_call x0 -> x4, Pallas kernels: none -> 50.4 us  [expert_grads(): pl.pallas_call(functools.partial(expert_kernel, count), out_shape=[jax.Sh...]
    ppermute x1 -> x42, starting transfers between devices: 4.08 us -> 36.2 us  [the longest x32 27.7 us: across(): return lax.ppermute(value, 'wide', pairs)]
    unnamed x47 -> x79, local copies, waits for them, and re-layouts: 12.6 us -> 35.1 us
  transfers between devices with their start and end apart: 10 -> 48, of which waited for: 9 -> 19; matrix products, arithmetic and copies ran while one was open for 18% -> 14% of each run, Pallas kernels for 0% -> 11%
where the time goes in v1:
time: 468 us; the launch traced here: 463 us
  waiting for transfers between devices  178 us (38%)
  blocking collectives  83 us (18%)
  Pallas kernels  50.4 us (11%)
  local copies, waits for them, and re-layouts  44.1 us (9%)
  matrix products  39.8 us (9%)
  starting transfers between devices  37 us (8%)
  between operations  15.8 us (3%)
  other arithmetic  15.4 us (3%)
    all_gather x1, blocking collectives, routed_sum(): dense_all = lax.all_gather(dense, ('wide', 'narrow'), axis=0, tiled=True)  71.6 us
    reduce_scatter x2, waiting for transfers between devices, on_device(): lax.psum_scatter(part.astype(jnp.bfloat16), 'wide', scatter_dimension=0,...  68.9 us
    pallas_call x4, Pallas kernels, expert_grads(): pl.pallas_call(functools.partial(expert_kernel, count), out_shape=[jax.Sh...  50.4 us
    ppermute x10, waiting for transfers between devices, along(): lax.ppermute(value, 'narrow', [(i, (i + 1) % size) for i in range(size)])  48.7 us
    unnamed x79, local copies, waits for them, and re-layouts  35.1 us
    ppermute x32, starting transfers between devices, across(): return lax.ppermute(value, 'wide', pairs)  27.7 us
    reduce_scatter x1, waiting for transfers between devices, on_device(): lax.psum_scatter(block_latent.astype(jnp.bfloat16), 'narrow', scatter_dim...  18.6 us
    all_gather x1, waiting for transfers between devices, on_device(): lax.all_gather(resid_grad, 'narrow', axis=0, tiled=True)  15.1 us
  transfers between devices with their start and end apart: 48, of which 19 were waited for; matrix products, arithmetic and copies ran while one was open for 14% of the time, Pallas kernels for 11%

profile of v1, /device:TPU:0, one launch (start us, length us, event | category | flops | bytes accessed | tf_op | source)
XLA Modules:
  0.0 463.1 jit_solution(5658567038057811359)
XLA Ops:
  11.0 3.0 collective-permute-start.10
  17.9 71.6 %all-gather = f32[32,64,16]{1,2,0:T(8,128)S(1)} all-gather(f32[1,64,16]{1,2,0:T(8,128)S(1)} %bitcast.127), channel_id=1, replica_groups=mesh['wide'=8,'narrow'=4] {'wide','narrow'}, dimensions={0}, use_global_device_ids=true | all-gather | bytes 135168 | tf_op jit(solution)/shard_map/all_gather | solution.py:122
  90.7 4.6 copy.88
  95.3 4.7 %copy.89 = bf16[1,2048,704]{2,1,0:T(8,128)(2,1)} copy(bf16[1,2048,704]{1,2,0:T(8,128)(2,1)} %param.22) | data formatting | bytes 5767168 | tf_op args[6]
  117.7 11.3 %collective-permute-done.11 = bf16[128,2048]{1,0:T(8,128)(2,1)S(1)} collective-permute-done((bf16[128,2048]{1,0:T(8,128)(2,1)}, bf16[128,2048]{1,0:T(8,128)(2,1)S(1)}, u32[]{:S(2)}, u32[]{:S(2)}) %collective-permute-start.11) | collective-permute-done | bytes 524320 | tf_op jit(solution)/shard_map/ppermute | solution.py:28
  130.9 9.3 %collective-permute-done.21 = bf16[128,2048]{1,0:T(8,128)(2,1)S(1)} collective-permute-done((bf16[128,2048]{1,0:T(8,128)(2,1)S(1)}, bf16[128,2048]{1,0:T(8,128)(2,1)S(1)}, u32[]{:S(2)}, u32[]{:S(2)}) %collective-permute-start.21) | collective-permute-done | bytes 524320 | tf_op jit(solution)/shard_map/ppermute | solution.py:28
  140.7 9.5 %collective-permute-done.12 = bf16[128,2048]{1,0:T(8,128)(2,1)S(1)} collective-permute-done((bf16[128,2048]{1,0:T(8,128)(2,1)S(1)}, bf16[128,2048]{1,0:T(8,128)(2,1)S(1)}, u32[]{:S(2)}, u32[]{:S(2)}) %collective-permute-start.12) | collective-permute-done | bytes 524320 | tf_op jit(solution)/shard_map/ppermute | solution.py:28
  152.7 3.2 collective-permute-done.22
  156.0 3.5 collective-permute-done.13
  165.6 13.0 %shard_map.191 = (bf16[256,2048]{1,0:T(8,128)(2,1)S(1)}, bf16[256,2048]{1,0:T(8,128)(2,1)}) custom-call(f32[512,1]{1,0:T(8,128)S(1)} %reshape.230.gate_ref, bf16[4,2,64,2048]{3,2,1,0:T(8,128)(2,1)} %bitcast.2.refs_0_, bf16[4,2,64,2048]{3,2,1,0:T(8,128)(2,1)S(1)} %bitcast.108, bf16[2048,704]{1,0:T(8,128)(2,1)S(1)} %bitcast.97, bf16[2048,704]{1,0:T(8,128)(2,1)} %bitcast.111, ...), custom_call_target="tpu_custom_call" | custom-call | flops 7381975040 | bytes 14942208 | tf_op jit(solution)/shard_map/pallas_call | solution.py:102
  181.0 12.2 %shard_map.194 = (bf16[256,2048]{1,0:T(8,128)(2,1)S(1)}, bf16[256,2048]{1,0:T(8,128)(2,1)S(1)}) custom-call(f32[512,1]{1,0:T(8,128)S(1)} %reshape.233.gate_ref, bf16[4,2,64,2048]{3,2,1,0:T(8,128)(2,1)S(1)} %bitcast.101, bf16[4,2,64,2048]{3,2,1,0:T(8,128)(2,1)} %bitcast.15.refs_1_, bf16[2048,704]{1,0:T(8,128)(2,1)S(1)} %bitcast.98, ...), custom_call_target="tpu_custom_call" | custom-call | flops 7381975040 | bytes 14942208 | tf_op jit(solution)/shard_map/pallas_call | solution.py:102
  194.6 2.5 collective-permute-start.6
  197.1 12.0 %shard_map.193 = (bf16[256,2048]{1,0:T(8,128)(2,1)S(1)}, bf16[256,2048]{1,0:T(8,128)(2,1)S(1)}) custom-call(f32[512,1]{1,0:T(8,128)S(1)} %reshape.232.gate_ref, bf16[4,2,64,2048]{3,2,1,0:T(8,128)(2,1)S(1)} %bitcast.103, bf16[4,2,64,2048]{3,2,1,0:T(8,128)(2,1)} %bitcast.12.refs_1_, bf16[2048,704]{1,0:T(8,128)(2,1)S(1)} %bitcast.99, ...), custom_call_target="tpu_custom_call" | custom-call | flops 7381975040 | bytes 14942208 | tf_op jit(solution)/shard_map/pallas_call | solution.py:102
  212.5 13.2 %shard_map.192 = (bf16[256,2048]{1,0:T(8,128)(2,1)S(1)}, bf16[256,2048]{1,0:T(8,128)(2,1)}) custom-call(f32[512,1]{1,0:T(8,128)S(1)} %reshape.231.gate_ref, bf16[4,2,64,2048]{3,2,1,0:T(8,128)(2,1)S(1)} %bitcast.102, bf16[4,2,64,2048]{3,2,1,0:T(8,128)(2,1)} %bitcast.9.refs_1_, bf16[2048,704]{1,0:T(8,128)(2,1)S(1)} %bitcast.100, bf16[2048,704]{1,0:T(8,128)(2,1)} %bitcast.114, ...), custom_call_target="tpu_custom_call" | custom-call | flops 7381975040 | bytes 14942208 | tf_op jit(solution)/shard_map/pallas_call | solution.py:102
  231.4 11.4 %all_gather.14 = bf16[2048,64]{0,1:T(8,128)(2,1)S(1)} all-gather(bf16[256,64]{0,1:T(8,128)(2,1)S(1)} %copy-done.22), channel_id=1, replica_groups=mesh['wide'=8,'narrow'=4] {'wide'}, dimensions={0}, use_global_device_ids=true | all-gather | bytes 294912 | tf_op jit(solution)/shard_map/all_gather | solution.py:211
  247.5 3.6 collective-permute-start.30
  252.7 9.9 %collective-permute-done.30 = bf16[64,2048]{1,0:T(8,128)(2,1)S(1)} collective-permute-done((bf16[64,2048]{1,0:T(8,128)(2,1)S(1)}, bf16[64,2048]{1,0:T(8,128)(2,1)S(1)}, u32[]{:S(2)}, u32[]{:S(2)}) %collective-permute-start.30) | collective-permute-done | bytes 262176 | tf_op jit(solution)/shard_map/ppermute | solution.py:28
  265.5 2.3 collective-permute-done.31
  273.4 4.9 %collective-permute-done.34 = bf16[64,2048]{1,0:T(8,128)(2,1)S(1)} collective-permute-done((bf16[64,2048]{1,0:T(8,128)(2,1)S(1)}, bf16[64,2048]{1,0:T(8,128)(2,1)S(1)}, u32[]{:S(2)}, u32[]{:S(2)}) %collective-permute-start.34) | collective-permute-done | bytes 262176 | tf_op jit(solution)/shard_map/ppermute | solution.py:23
  282.0 5.6 %collective-permute-done.41 = bf16[64,2048]{1,0:T(8,128)(2,1)S(1)} collective-permute-done((bf16[64,2048]{1,0:T(8,128)(2,1)S(1)}, bf16[64,2048]{1,0:T(8,128)(2,1)S(1)}, u32[]{:S(2)}, u32[]{:S(2)}) %collective-permute-start.41) | collective-permute-done | bytes 262176 | tf_op jit(solution)/shard_map/ppermute | solution.py:28
  289.9 4.3 fusion.12
  294.2 2.6 fusion.35
  300.2 15.1 %all-gather.6.cloned.1.call-done = bf16[256,2048]{1,0:T(8,128)(2,1)} async-done(((bf16[64,2048]{1,0:T(8,128)(2,1)}), bf16[256,2048]{1,0:T(8,128)(2,1)}) %all-gather.6.cloned.1.call-update) | async-done | bytes 1048592 | tf_op jit(solution)/shard_map/all_gather | solution.py:204
  317.8 8.4 %fusion.3 = f32[2048,512,1]{1,0,2:T(8,128)} fusion(bf16[4,256,512]{2,1,0:T(8,128)(2,1)S(1)} %convolution_convert_fusion, f32[4,256,2048]{2,1,0:T(8,128)} %copy-done.6, f32[4,256]{1,0:T(4,128)S(1)} %log_add_fusion), kind=kOutput, calls=%fused_computation.12 | convolution fusion | flops 2151677952 | bytes 13635584 | tf_op jit(solution)/shard_map/hts,htl->sl/dot_general | solution.py:254
  326.1 3.0 multiply_reduce_fusion
  335.0 7.2 %fusion.5 = bf16[2048,512]{1,0:T(8,128)(2,1)} fusion(f32[2048,512,1]{1,0,2:T(8,128)} %fusion.3, bf16[4,256,2048]{2,1,0:T(8,128)(2,1)} %copy-done.7, bf16[4,256,512]{2,1,0:T(8,128)(2,1)S(1)} %copy-done.12), kind=kOutput, calls=%fused_computation.14 | convolution fusion | flops 2149580800 | bytes 11534336 | tf_op jit(solution)/shard_map/hts,htl->sl/dot_general | solution.py:257
  342.3 25.8 %reduce-scatter.11.cloned.1.call-done = bf16[256,64]{0,1:T(8,128)(2,1)} async-done(((bf16[2048,64]{0,1:T(8,128)(2,1)}), bf16[256,64]{0,1:T(8,128)(2,1)}) %reduce-scatter.11.cloned.1.call-update) | async-done | bytes 32784 | tf_op jit(solution)/shard_map/reduce_scatter | solution.py:262
  369.6 43.2 %reduce-scatter.7.cloned.1.call-done = bf16[256,512]{1,0:T(8,128)(2,1)} async-done(((bf16[2048,512]{1,0:T(8,128)(2,1)}), bf16[256,512]{1,0:T(8,128)(2,1)}) %reduce-scatter.7.cloned.1.call-update) | async-done | bytes 262160 | tf_op jit(solution)/shard_map/reduce_scatter | solution.py:262
  412.8 5.5 %fusion.20 = bf16[4,256,128]{1,2,0:T(8,128)(2,1)S(1)} fusion(bf16[4,128,512]{2,1,0:T(8,128)(2,1)S(1)} %bitcast.120, bf16[4,256,2048]{2,1,0:T(8,128)(2,1)} %copy-done.7, bf16[2048,512]{1,0:T(8,128)(2,1)} %all-gather.4.cloned.1.call-done), kind=kOutput, calls=%fused_computation.32 | convolution fusion | flops 2282356736 | bytes 7077888 | tf_op jit(solution)/shard_map/htl,hnl->thn/dot_general | solution.py:248
  419.1 3.6 convolution_convert_fusion.3
  423.5 11.0 %reduce-scatter.13.cloned.1.call-done = bf16[64,64]{1,0:T(8,128)(2,1)} async-done(((bf16[256,64]{1,0:T(8,128)(2,1)}), bf16[64,64]{1,0:T(8,128)(2,1)}) %reduce-scatter.13.cloned.1.call-update) | async-done | bytes 8208
  436.0 18.6 %reduce-scatter.9.cloned.1.call-done = bf16[64,512]{1,0:T(8,128)(2,1)} async-done(((bf16[256,512]{1,0:T(8,128)(2,1)}), bf16[64,512]{1,0:T(8,128)(2,1)}) %reduce-scatter.9.cloned.1.call-update) | async-done | bytes 65552 | tf_op jit(solution)/shard_map/reduce_scatter | solution.py:268
  (220 shorter events, 87.9 us)
Async XLA Ops:
  7.2 282.7 %all-gather.4.cloned.1.call-start = ((), (), s32[]{:S(2)}) async-start(), calls=%async_computation.4 | async-start | bytes 2359296 | tf_op jit(solution)/shard_map/all_gather | solution.py:210
  11.0 97.4 %collective-permute-start.10 = (bf16[128,2048]{1,0:T(8,128)(2,1)}, bf16[128,2048]{1,0:T(8,128)(2,1)}, u32[]{:S(2)}, u32[]{:S(2)}) collective-permute-start(bf16[128,2048]{1,0:T(8,128)(2,1)} %get-tuple-element.64), channel_id=1, source_target_pairs={{0,1},{1,2},{2,3},{3,0},{4,5},{5,6},{6,7},{7,4},{8,9},{9,10},{10,1... | collective-permute-start | bytes 1572872 | tf_op jit(solution)/shard_map/ppermute | solution.py:28
  14.0 90.7 %collective-permute-start.1 = (bf16[128,2048]{1,0:T(8,128)(2,1)}, bf16[128,2048]{1,0:T(8,128)(2,1)}, u32[]{:S(2)}, u32[]{:S(2)}) collective-permute-start(bf16[128,2048]{1,0:T(8,128)(2,1)} %get-tuple-element.64), channel_id=1, source_target_pairs={{0,16},{4,20},{8,24},{12,28},{16,0},{20,4},{24,8},{28,12},{1,17},{... | collective-permute-start | bytes 1572872 | tf_op jit(solution)/shard_map/ppermute | solution.py:23
  15.6 90.3 %collective-permute-start = (bf16[128,2048]{1,0:T(8,128)(2,1)}, bf16[128,2048]{1,0:T(8,128)(2,1)}, u32[]{:S(2)}, u32[]{:S(2)}) collective-permute-start(bf16[128,2048]{1,0:T(8,128)(2,1)} %get-tuple-element.64), channel_id=1, source_target_pairs={{0,8},{4,12},{8,0},{12,4},{16,24},{20,28},{24,16},{28,20},{1,9},{5... | collective-permute-start | bytes 1572872 | tf_op jit(solution)/shard_map/ppermute | solution.py:23
  17.1 298.2 %all-gather.6.cloned.1.call-start = ((), (), s32[]{:S(2)}) async-start(), calls=%async_computation.5 | async-start | bytes 1310720 | tf_op jit(solution)/shard_map/all_gather | solution.py:204
  109.5 19.6 %collective-permute-start.25 = (bf16[128,2048]{1,0:T(8,128)(2,1)}, bf16[128,2048]{1,0:T(8,128)(2,1)S(1)}, u32[]{:S(2)}, u32[]{:S(2)}) collective-permute-start(bf16[128,2048]{1,0:T(8,128)(2,1)} %collective-permute-done.10), channel_id=1, source_target_pairs={{0,8},{4,12},{8,0},{12,4},{16,24},{20,28},{24,16},{28,20},{1,9},{5... | collective-permute-start | bytes 1572872 | tf_op jit(solution)/shard_map/ppermute | solution.py:23
  111.6 17.6 %collective-permute-start.26 = (bf16[128,2048]{1,0:T(8,128)(2,1)}, bf16[128,2048]{1,0:T(8,128)(2,1)S(1)}, u32[]{:S(2)}, u32[]{:S(2)}) collective-permute-start(bf16[128,2048]{1,0:T(8,128)(2,1)} %collective-permute-done.10), channel_id=1, source_target_pairs={{0,16},{4,20},{8,24},{12,28},{16,0},{20,4},{24,8},{28,12},{1,17},{... | collective-permute-start | bytes 1572872 | tf_op jit(solution)/shard_map/ppermute | solution.py:23
  112.1 16.9 %collective-permute-start.11 = (bf16[128,2048]{1,0:T(8,128)(2,1)}, bf16[128,2048]{1,0:T(8,128)(2,1)S(1)}, u32[]{:S(2)}, u32[]{:S(2)}) collective-permute-start(bf16[128,2048]{1,0:T(8,128)(2,1)} %collective-permute-done.10), channel_id=1, source_target_pairs={{0,1},{1,2},{2,3},{3,0},{4,5},{5,6},{6,7},{7,4},{8,9},{9,10},{10,1... | collective-permute-start | bytes 1572872 | tf_op jit(solution)/shard_map/ppermute | solution.py:28
  116.2 24.0 %collective-permute-start.21 = (bf16[128,2048]{1,0:T(8,128)(2,1)S(1)}, bf16[128,2048]{1,0:T(8,128)(2,1)S(1)}, u32[]{:S(2)}, u32[]{:S(2)}) collective-permute-start(bf16[128,2048]{1,0:T(8,128)(2,1)S(1)} %pad_maximum_fusion), channel_id=1, source_target_pairs={{0,1},{1,2},{2,3},{3,0},{4,5},{5,6},{6,7},{7,4},{8,9},{9,10},{10,1... | collective-permute-start | bytes 1572872 | tf_op jit(solution)/shard_map/ppermute | solution.py:28
  117.7 45.0 %collective-permute-start.4 = (bf16[512,2048]{1,0:T(8,128)(2,1)}, bf16[512,2048]{1,0:T(8,128)(2,1)S(1)}, u32[]{:S(2)}, u32[]{:S(2)}) collective-permute-start(bf16[512,2048]{1,0:T(8,128)(2,1)} %constant_dynamic-update-slice_fusion.2), channel_id=1, source_target_pairs={{0,4},{4,0},{8,12},{12,8},{16,20},{20,16},{24,28},{28,24},{1,5},{5... | collective-permute-start | bytes 6291464 | tf_op jit(solution)/shard_map/ppermute | solution.py:23
  129.0 22.6 %collective-permute-start.19 = (bf16[128,2048]{1,0:T(8,128)(2,1)S(1)}, bf16[128,2048]{1,0:T(8,128)(2,1)S(1)}, u32[]{:S(2)}, u32[]{:S(2)}) collective-permute-start(bf16[128,2048]{1,0:T(8,128)(2,1)S(1)} %collective-permute-done.11), channel_id=1, source_target_pairs={{0,8},{4,12},{8,0},{12,4},{16,24},{20,28},{24,16},{28,20},{1,9},{5... | collective-permute-start | bytes 1572872 | tf_op jit(solution)/shard_map/ppermute | solution.py:23
  129.1 21.1 %collective-permute-start.12 = (bf16[128,2048]{1,0:T(8,128)(2,1)S(1)}, bf16[128,2048]{1,0:T(8,128)(2,1)S(1)}, u32[]{:S(2)}, u32[]{:S(2)}) collective-permute-start(bf16[128,2048]{1,0:T(8,128)(2,1)S(1)} %collective-permute-done.11), channel_id=1, source_target_pairs={{0,1},{1,2},{2,3},{3,0},{4,5},{5,6},{6,7},{7,4},{8,9},{9,10},{10,1... | collective-permute-start | bytes 1572872 | tf_op jit(solution)/shard_map/ppermute | solution.py:28
  129.2 23.3 %collective-permute-start.20 = (bf16[128,2048]{1,0:T(8,128)(2,1)S(1)}, bf16[128,2048]{1,0:T(8,128)(2,1)S(1)}, u32[]{:S(2)}, u32[]{:S(2)}) collective-permute-start(bf16[128,2048]{1,0:T(8,128)(2,1)S(1)} %collective-permute-done.11), channel_id=1, source_target_pairs={{0,16},{4,20},{8,24},{12,28},{16,0},{20,4},{24,8},{28,12},{1,17},{... | collective-permute-start | bytes 1572872 | tf_op jit(solution)/shard_map/ppermute | solution.py:23
  140.2 15.7 %collective-permute-start.22 = (bf16[128,2048]{1,0:T(8,128)(2,1)S(1)}, bf16[128,2048]{1,0:T(8,128)(2,1)S(1)}, u32[]{:S(2)}, u32[]{:S(2)}) collective-permute-start(bf16[128,2048]{1,0:T(8,128)(2,1)S(1)} %collective-permute-done.21), channel_id=1, source_target_pairs={{0,1},{1,2},{2,3},{3,0},{4,5},{5,6},{6,7},{7,4},{8,9},{9,10},{10,1... | collective-permute-start | bytes 1572872 | tf_op jit(solution)/shard_map/ppermute | solution.py:28
  152.5 26.7 %collective-permute-start.27 = (bf16[512,2048]{1,0:T(8,128)(2,1)S(1)}, bf16[512,2048]{1,0:T(8,128)(2,1)}, u32[]{:S(2)}, u32[]{:S(2)}) collective-permute-start(bf16[512,2048]{1,0:T(8,128)(2,1)S(1)} %constant_dynamic-update-slice_fusion.17), channel_id=1, source_target_pairs={{0,4},{4,0},{8,12},{12,8},{16,20},{20,16},{24,28},{28,24},{1,5},{5... | collective-permute-start | bytes 6291464 | tf_op jit(solution)/shard_map/ppermute | solution.py:23
  155.9 41.2 %collective-permute-start.23 = (bf16[512,2048]{1,0:T(8,128)(2,1)S(1)}, bf16[512,2048]{1,0:T(8,128)(2,1)}, u32[]{:S(2)}, u32[]{:S(2)}) collective-permute-start(bf16[512,2048]{1,0:T(8,128)(2,1)S(1)} %constant_dynamic-update-slice_fusion.13), channel_id=1, source_target_pairs={{0,4},{4,0},{8,12},{12,8},{16,20},{20,16},{24,28},{28,24},{1,5},{5... | collective-permute-start | bytes 6291464 | tf_op jit(solution)/shard_map/ppermute | solution.py:23
  159.5 19.0 %collective-permute-start.15 = (bf16[64,2048]{1,0:T(8,128)(2,1)S(1)}, bf16[64,2048]{1,0:T(8,128)(2,1)S(1)}, u32[]{:S(2)}, u32[]{:S(2)}) collective-permute-start(bf16[64,2048]{1,0:T(8,128)(2,1)S(1)} %slice.106), channel_id=1, source_target_pairs={{0,16},{4,20},{8,24},{12,28},{16,0},{20,4},{24,8},{28,12},{1,17},{... | collective-permute-start | bytes 786440 | tf_op jit(solution)/shard_map/ppermute | solution.py:23
  162.4 16.2 %collective-permute-start.16 = (bf16[64,2048]{1,0:T(8,128)(2,1)S(1)}, bf16[64,2048]{1,0:T(8,128)(2,1)S(1)}, u32[]{:S(2)}, u32[]{:S(2)}) collective-permute-start(bf16[64,2048]{1,0:T(8,128)(2,1)S(1)} %slice.107), channel_id=1, source_target_pairs={{0,8},{4,12},{8,0},{12,4},{16,24},{20,28},{24,16},{28,20},{1,9},{5... | collective-permute-start | bytes 786440 | tf_op jit(solution)/shard_map/ppermute | solution.py:23
  178.6 33.1 %collective-permute-start.17 = (bf16[512,2048]{1,0:T(8,128)(2,1)S(1)}, bf16[512,2048]{1,0:T(8,128)(2,1)}, u32[]{:S(2)}, u32[]{:S(2)}) collective-permute-start(bf16[512,2048]{1,0:T(8,128)(2,1)S(1)} %constant_dynamic-update-slice_fusion.8), channel_id=1, source_target_pairs={{0,4},{4,0},{8,12},{12,8},{16,20},{20,16},{24,28},{28,24},{1,5},{5... | collective-permute-start | bytes 6291464 | tf_op jit(solution)/shard_map/ppermute | solution.py:23
  193.2 16.1 %collective-permute-start.28 = (bf16[256,2048]{1,0:T(8,128)(2,1)S(1)}, bf16[256,2048]{1,0:T(8,128)(2,1)S(1)}, u32[]{:S(2)}, u32[]{:S(2)}) collective-permute-start(bf16[256,2048]{1,0:T(8,128)(2,1)S(1)} %get-tuple-element.20), channel_id=1, source_target_pairs={{0,4},{4,0},{8,12},{12,8},{16,20},{20,16},{24,28},{28,24},{1,5},{5... | collective-permute-start | bytes 3145736 | tf_op jit(solution)/shard_map/ppermute | solution.py:23
  194.6 34.4 %collective-permute-start.6 = (bf16[64,1024]{1,0:T(8,128)(2,1)S(1)}, bf16[64,1024]{1,0:T(8,128)(2,1)S(1)}, u32[]{:S(2)}, u32[]{:S(2)}) collective-permute-start(bf16[64,1024]{1,0:T(8,128)(2,1)S(1)} %get-tuple-element.48), channel_id=1, source_target_pairs={{0,16},{4,20},{8,24},{12,28},{16,0},{20,4},{24,8},{28,12},{1,17},{... | collective-permute-start | bytes 393224 | tf_op jit(solution)/shard_map/ppermute | solution.py:23
  197.0 33.7 %collective-permute-start.8 = (bf16[64,1024]{1,0:T(8,128)(2,1)S(1)}, bf16[64,1024]{1,0:T(8,128)(2,1)S(1)}, u32[]{:S(2)}, u32[]{:S(2)}) collective-permute-start(bf16[64,1024]{1,0:T(8,128)(2,1)S(1)} %get-tuple-element.49), channel_id=1, source_target_pairs={{0,8},{4,12},{8,0},{12,4},{16,24},{20,28},{24,16},{28,20},{1,9},{5... | collective-permute-start | bytes 393224 | tf_op jit(solution)/shard_map/ppermute | solution.py:23
  209.1 17.5 %collective-permute-start.24 = (bf16[256,2048]{1,0:T(8,128)(2,1)S(1)}, bf16[256,2048]{1,0:T(8,128)(2,1)S(1)}, u32[]{:S(2)}, u32[]{:S(2)}) collective-permute-start(bf16[256,2048]{1,0:T(8,128)(2,1)S(1)} %get-tuple-element.18), channel_id=1, source_target_pairs={{0,4},{4,0},{8,12},{12,8},{16,20},{20,16},{24,28},{28,24},{1,5},{5... | collective-permute-start | bytes 3145736 | tf_op jit(solution)/shard_map/ppermute | solution.py:23
  225.7 25.3 %collective-permute-start.18 = (bf16[256,2048]{1,0:T(8,128)(2,1)}, bf16[256,2048]{1,0:T(8,128)(2,1)}, u32[]{:S(2)}, u32[]{:S(2)}) collective-permute-start(bf16[256,2048]{1,0:T(8,128)(2,1)} %get-tuple-element.16), channel_id=1, source_target_pairs={{0,4},{4,0},{8,12},{12,8},{16,20},{20,16},{24,28},{28,24},{1,5},{5... | collective-permute-start | bytes 3145736 | tf_op jit(solution)/shard_map/ppermute | solution.py:23
  225.8 19.3 %collective-permute-start.29 = (bf16[64,2048]{1,0:T(8,128)(2,1)}, bf16[64,2048]{1,0:T(8,128)(2,1)}, u32[]{:S(2)}, u32[]{:S(2)}) collective-permute-start(bf16[64,2048]{1,0:T(8,128)(2,1)} %get-tuple-element.58), channel_id=1, source_target_pairs={{0,1},{1,2},{2,3},{3,0},{4,5},{5,6},{6,7},{7,4},{8,9},{9,10},{10,1... | collective-permute-start | bytes 786440 | tf_op jit(solution)/shard_map/ppermute | solution.py:28
  226.6 18.4 %collective-permute-start.39 = (bf16[64,2048]{1,0:T(8,128)(2,1)}, bf16[64,2048]{1,0:T(8,128)(2,1)}, u32[]{:S(2)}, u32[]{:S(2)}) collective-permute-start(bf16[64,2048]{1,0:T(8,128)(2,1)} %add_convert_fusion.7), channel_id=1, source_target_pairs={{0,1},{1,2},{2,3},{3,0},{4,5},{5,6},{6,7},{7,4},{8,9},{9,10},{10,1... | collective-permute-start | bytes 786440 | tf_op jit(solution)/shard_map/ppermute | solution.py:28
  228.9 16.1 %collective-permute-start.36 = (bf16[64,2048]{1,0:T(8,128)(2,1)}, bf16[64,2048]{1,0:T(8,128)(2,1)}, u32[]{:S(2)}, u32[]{:S(2)}) collective-permute-start(bf16[64,2048]{1,0:T(8,128)(2,1)} %get-tuple-element.62), channel_id=1, source_target_pairs={{0,16},{4,20},{8,24},{12,28},{16,0},{20,4},{24,8},{28,12},{1,17},{... | collective-permute-start | bytes 786440 | tf_op jit(solution)/shard_map/ppermute | solution.py:23
  246.6 26.8 %collective-permute-start.40 = (bf16[64,2048]{1,0:T(8,128)(2,1)S(1)}, bf16[64,2048]{1,0:T(8,128)(2,1)S(1)}, u32[]{:S(2)}, u32[]{:S(2)}) collective-permute-start(bf16[64,2048]{1,0:T(8,128)(2,1)S(1)} %get-tuple-element.57), channel_id=1, source_target_pairs={{0,1},{1,2},{2,3},{3,0},{4,5},{5,6},{6,7},{7,4},{8,9},{9,10},{10,1... | collective-permute-start | bytes 786440 | tf_op jit(solution)/shard_map/ppermute | solution.py:28
  289.4 78.6 %reduce-scatter.11.cloned.1.call-start = ((), (), s32[]{:S(2)}) async-start(), calls=%async_computation.8 | async-start | bytes 294912 | tf_op jit(solution)/shard_map/reduce_scatter | solution.py:262
  334.7 78.0 %reduce-scatter.7.cloned.1.call-start = ((), (), s32[]{:S(2)}) async-start(), calls=%async_computation.6 | async-start | bytes 2359296 | tf_op jit(solution)/shard_map/reduce_scatter | solution.py:262
  342.2 92.2 %reduce-scatter.13.cloned.1.call-start = ((), (), s32[]{:S(2)}) async-start(), calls=%async_computation.9 | async-start | bytes 81920
  369.5 85.0 %reduce-scatter.9.cloned.1.call-start = ((), (), s32[]{:S(2)}) async-start(), calls=%async_computation.7 | async-start | bytes 327680 | tf_op jit(solution)/shard_map/reduce_scatter | solution.py:268
  (43 other events, 814.1 us)
Sparse Core Ops, SparseCore 0:
  17.2 28.0 all-gather.3
  289.6 25.7 all-gather.5
  334.9 33.1 reduce-scatter.10
  371.5 41.2 reduce-scatter.6
  415.4 18.9 reduce-scatter.12
  436.6 17.8 reduce-scatter.8
